TPU v7x, 128 devices: a whole 4x4x4 slice. The times are simulated.
128 devices in a mesh: row: 16 (over y_hi, x, core), col: 8 (over z, y_lo).
Axes of the slice: x: 4, y: 4 (y_hi: 2, y_lo: 2; y = y_hi * 2 + y_lo), z: 4, core: 2. Of those that a mesh axis runs over, the one named last changes fastest.
Arguments:
- cycle_inter: float32 [1536, 1536, 128], P(None, ('row', 'col')), may hold values from -6 to 6
- integrals: float32 [1536, 1536, 128], P(None, ('row', 'col')), may hold values from -0.005859375 to 0.005859375
Outputs:
- ladder: float32 [128, 128], P('row')
All inputs are finite; a program needn't handle non-finite values.
Results may differ from a plain program's by a relative error of at most 0.0003.
Values sent between devices are 32-bit elements; how exact they have to be, the bound alone decides.
No kernel may reach another device: no remote copies, remote signals or barrier semaphores. Data moves between devices by JAX's collectives and lax.ppermute only.
A program may use at most 128 MiB of HBM per device.

v0:
```python
import jax
import jax.numpy as jnp
from jax import lax
from jax.sharding import PartitionSpec as P


def body(cycle_inter, integrals):
    row_count = lax.axis_size("row")
    col_count = lax.axis_size("col")
    local_width = cycle_inter.shape[1]
    occupied = cycle_inter.shape[2]
    slab_pairs = integrals.shape[2]
    received = lax.all_to_all(cycle_inter, ("row", "col"), split_axis=0, concat_axis=1, tiled=True)
    amplitudes = cycle_inter - jnp.swapaxes(received, 0, 1)
    device_rank = lax.axis_index("row") * col_count + lax.axis_index("col")
    first_column = device_rank * local_width
    column_ids = first_column + jnp.arange(local_width, dtype=jnp.int32)
    block_rows = 128
    needed_blocks = (first_column + local_width + block_rows - 1) // block_rows

    def accumulate(block_index, summed):
        offset = block_index * block_rows
        amp_block = lax.dynamic_slice_in_dim(amplitudes, offset, block_rows, 0)
        integral_block = lax.dynamic_slice_in_dim(integrals, offset, block_rows, 0)
        row_ids = offset + jnp.arange(block_rows, dtype=jnp.int32)
        upper_mask = (row_ids[:, None] < column_ids[None, :]).astype(jnp.float32)
        amp_block = amp_block * upper_mask[:, :, None]
        return summed + jnp.einsum(
            "cdi,cda->ia", amp_block, integral_block, precision=lax.Precision.HIGHEST
        )

    partial_sum = lax.fori_loop(
        0, needed_blocks, accumulate, jnp.zeros((occupied, slab_pairs), jnp.float32)
    )
    owned_rows = occupied // row_count
    summed = lax.psum(partial_sum, ("row", "col"))
    return lax.dynamic_slice_in_dim(summed, lax.axis_index("row") * owned_rows, owned_rows, 0)


def solution(mesh):
    return jax.shard_map(
        body,
        mesh=mesh,
        in_specs=(P(None, ("row", "col"), None), P(None, ("row", "col"), None)),
        out_specs=P("row", None),
        check_vma=False,
    )
```

profile of v0, /device:TPU:1, one launch (start us, length us, event | category | flops | bytes accessed | tf_op | source)
XLA Modules:
  0.0 412.1 jit_solution(1875631772332710024)
XLA Ops:
  6.5 12.7 %copy.7 = f32[1536,12,128]{2,1,0:T(8,128)} copy(f32[1536,12,128]{2,0,1:T(8,128)} %param.4) | data formatting | bytes 18874368 | tf_op args[0]
  19.2 11.9 %all-to-all-start = ((f32[1536,12,128]{2,1,0:T(8,128)}), f32[1536,12,128]{2,1,0:T(8,128)}, u32[]{:S(2)}, u32[]{:S(2)}) async-start(f32[1536,12,128]{2,1,0:T(8,128)} %copy.7), calls=%async_computation | async-start | bytes 25165824 | tf_op jit(solution)/shard_map/all_to_all | solution.py:13
  31.1 0.0 all-reduce.2.cloned.1.call-start
  31.2 165.2 %all-to-all-done = f32[1536,12,128]{2,1,0:T(8,128)} async-done(((f32[1536,12,128]{2,1,0:T(8,128)}), f32[1536,12,128]{2,1,0:T(8,128)}, u32[]{:S(2)}, u32[]{:S(2)}) %all-to-all-start) | async-done | bytes 9437216 | tf_op jit(solution)/shard_map/all_to_all | solution.py:13
  196.3 10.3 %copy.9 = f32[12,128,12,128]{3,2,1,0:T(8,128)} copy(f32[12,128,12,128]{3,2,0,1:T(8,128)} %bitcast.2) | data formatting | bytes 18874368 | tf_op jit(solution)/shard_map/all_to_all | solution.py:13
  206.7 12.0 %all_to_all.16 = f32[12,1536,128]{2,1,0:T(8,128)} reshape(f32[12,128,12,128]{3,2,1,0:T(8,128)} %copy.9) | data formatting | bytes 18874368 | tf_op jit(solution)/shard_map/all_to_all | solution.py:13
  218.7 10.9 %bitcast_subtract_fusion = f32[1536,12,128]{2,0,1:T(8,128)} fusion(f32[1536,12,128]{2,0,1:T(8,128)} %param.4, f32[12,1536,128]{2,1,0:T(8,128)} %all_to_all.16), kind=kLoop, calls=%fused_computation.11 | loop fusion | flops 2359296 | bytes 28311552 | tf_op jit(solution)/shard_map/sub | solution.py:14
  229.6 3.6 while.11
  229.6 1.2 constant_dynamic-slice_fusion.3
  230.8 0.3 copy.15
  231.1 0.1 compare_convert_fusion.2
  231.2 2.1 fusion.12
  233.2 0.0 copy-start
  233.2 0.6 copy-done
  233.9 0.0 all-reduce.2.cloned.1.call-update
  233.9 170.1 %all-reduce.2.cloned.1.call-done = f32[128,128]{1,0:T(8,128)} async-done(((f32[128,128]{1,0:T(8,128)}), f32[128,128]{1,0:T(8,128)}) %all-reduce.2.cloned.1.call-update) | async-done | bytes 65552 | tf_op jit(solution)/shard_map/psum | solution.py:36
  404.0 1.3 constant_dynamic-slice_fusion.1
  (3 shorter events, 0.0 us)
Async XLA Ops:
  19.2 177.2 %all-to-all-start = ((f32[1536,12,128]{2,1,0:T(8,128)}), f32[1536,12,128]{2,1,0:T(8,128)}, u32[]{:S(2)}, u32[]{:S(2)}) async-start(f32[1536,12,128]{2,1,0:T(8,128)} %copy.7), calls=%async_computation | async-start | bytes 25165824 | tf_op jit(solution)/shard_map/all_to_all | solution.py:13
  31.1 372.9 %all-reduce.2.cloned.1.call-start = ((), (), s32[]{:S(2)}) async-start(), calls=%async_computation.1 | async-start | bytes 131072 | tf_op jit(solution)/shard_map/psum | solution.py:36
  233.2 0.6 copy-start
Sparse Core Ops, SparseCore 0:
  234.0 169.9 all-reduce.1
where the time goes:
time: 414 us; the launch traced here: 412 us
  waiting for transfers between devices  335 us (81%)
  local copies, waits for them, and re-layouts  38.3 us (9%)
  between operations  13.4 us (3%)
  starting transfers between devices  11.9 us (3%)
  other arithmetic  11 us (3%)
    psum x1, waiting for transfers between devices, body(): summed = lax.psum(partial_sum, ('row', 'col'))  170 us
    all_to_all x1, waiting for transfers between devices, body(): lax.all_to_all(cycle_inter, ('row', 'col'), split_axis=0, concat_axis=1,...  165 us
    all_to_all x2, local copies, waits for them, and re-layouts, body(): lax.all_to_all(cycle_inter, ('row', 'col'), split_axis=0, concat_axis=1,...  22.3 us
    unnamed x3, local copies, waits for them, and re-layouts  13.3 us
    all_to_all x1, starting transfers between devices, body(): lax.all_to_all(cycle_inter, ('row', 'col'), split_axis=0, concat_axis=1,...  11.9 us
    sub x1, other arithmetic, body(): amplitudes = cycle_inter - jnp.swapaxes(received, 0, 1)  10.9 us
  transfers between devices with their start and end apart: 2, of which 2 were waited for; matrix products, arithmetic and copies ran while one was open for 0% of the time, Pallas kernels for 0%

commit v1 on v0

--- a/solution.py
+++ b/solution.py
@@ -33,7 +33,7 @@
         0, needed_blocks, accumulate, jnp.zeros((occupied, slab_pairs), jnp.float32)
     )
     owned_rows = occupied // row_count
-    summed = lax.psum(partial_sum, ("row", "col"))
+    summed = lax.psum(lax.psum(partial_sum, "row"), "col")
     return lax.dynamic_slice_in_dim(summed, lax.axis_index("row") * owned_rows, owned_rows, 0)
 
 

time: 414 us -> 478 us (1.15)
  waiting for transfers between devices: 335 us -> 395 us
    psum x1 -> x2, waiting for transfers between devices: 170 us -> 230 us  [body(): summed = lax.psum(lax.psum(partial_sum, 'row'), 'col')]
  transfers between devices with their start and end apart: 2 -> 3, of which waited for: 2 -> 3; matrix products, arithmetic and copies ran while one was open for 0% -> 0% of each run, Pallas kernels for 0% -> 0%
where the time goes in v1:
time: 478 us; the launch traced here: 472 us
  waiting for transfers between devices  395 us (83%)
  local copies, waits for them, and re-layouts  38.3 us (8%)
  between operations  13.4 us (3%)
  starting transfers between devices  12 us (3%)
  other arithmetic  11 us (2%)
    psum x2, waiting for transfers between devices, body(): summed = lax.psum(lax.psum(partial_sum, 'row'), 'col')  230 us
    all_to_all x1, waiting for transfers between devices, body(): lax.all_to_all(cycle_inter, ('row', 'col'), split_axis=0, concat_axis=1,...  165 us
    all_to_all x2, local copies, waits for them, and re-layouts, body(): lax.all_to_all(cycle_inter, ('row', 'col'), split_axis=0, concat_axis=1,...  22.3 us
    unnamed x3, local copies, waits for them, and re-layouts  13.3 us
    all_to_all x1, starting transfers between devices, body(): lax.all_to_all(cycle_inter, ('row', 'col'), split_axis=0, concat_axis=1,...  11.9 us
    sub x1, other arithmetic, body(): amplitudes = cycle_inter - jnp.swapaxes(received, 0, 1)  10.9 us
  transfers between devices with their start and end apart: 3, of which 3 were waited for; matrix products, arithmetic and copies ran while one was open for 0% of the time, Pallas kernels for 0%

profile of v1, /device:TPU:1, one launch (start us, length us, event | category | flops | bytes accessed | tf_op | source)
XLA Modules:
  0.0 471.9 jit_solution(12249380873708650889)
XLA Ops:
  6.5 12.7 %copy.7 = f32[1536,12,128]{2,1,0:T(8,128)} copy(f32[1536,12,128]{2,0,1:T(8,128)} %param.4) | data formatting | bytes 18874368 | tf_op args[0]
  19.2 11.9 %all-to-all-start = ((f32[1536,12,128]{2,1,0:T(8,128)}), f32[1536,12,128]{2,1,0:T(8,128)}, u32[]{:S(2)}, u32[]{:S(2)}) async-start(f32[1536,12,128]{2,1,0:T(8,128)} %copy.7), calls=%async_computation | async-start | bytes 25165824 | tf_op jit(solution)/shard_map/all_to_all | solution.py:13
  31.1 0.0 all-reduce.3.cloned.1.call-start
  31.2 165.2 %all-to-all-done = f32[1536,12,128]{2,1,0:T(8,128)} async-done(((f32[1536,12,128]{2,1,0:T(8,128)}), f32[1536,12,128]{2,1,0:T(8,128)}, u32[]{:S(2)}, u32[]{:S(2)}) %all-to-all-start) | async-done | bytes 9437216 | tf_op jit(solution)/shard_map/all_to_all | solution.py:13
  196.3 10.3 %copy.9 = f32[12,128,12,128]{3,2,1,0:T(8,128)} copy(f32[12,128,12,128]{3,2,0,1:T(8,128)} %bitcast.2) | data formatting | bytes 18874368 | tf_op jit(solution)/shard_map/all_to_all | solution.py:13
  206.7 12.0 %all_to_all.16 = f32[12,1536,128]{2,1,0:T(8,128)} reshape(f32[12,128,12,128]{3,2,1,0:T(8,128)} %copy.9) | data formatting | bytes 18874368 | tf_op jit(solution)/shard_map/all_to_all | solution.py:13
  218.7 10.9 %bitcast_subtract_fusion = f32[1536,12,128]{2,0,1:T(8,128)} fusion(f32[1536,12,128]{2,0,1:T(8,128)} %param.4, f32[12,1536,128]{2,1,0:T(8,128)} %all_to_all.16), kind=kLoop, calls=%fused_computation.11 | loop fusion | flops 2359296 | bytes 28311552 | tf_op jit(solution)/shard_map/sub | solution.py:14
  229.6 3.6 while.11
  229.6 1.2 constant_dynamic-slice_fusion.3
  230.8 0.3 copy.15
  231.1 0.1 compare_convert_fusion.2
  231.2 2.1 fusion.12
  233.2 0.0 copy-start
  233.2 0.6 copy-done
  233.9 0.0 all-reduce.3.cloned.1.call-update
  233.9 0.0 all-reduce.5.cloned.1.call-start
  233.9 158.1 %all-reduce.3.cloned.1.call-done = f32[128,128]{1,0:T(8,128)} async-done(((f32[128,128]{1,0:T(8,128)}), f32[128,128]{1,0:T(8,128)}) %all-reduce.3.cloned.1.call-update) | async-done | bytes 65552 | tf_op jit(solution)/shard_map/psum | solution.py:36
  392.1 0.0 all-reduce.5.cloned.1.call-update
  392.1 71.7 %all-reduce.5.cloned.1.call-done = f32[128,128]{1,0:T(8,128)} async-done(((f32[128,128]{1,0:T(8,128)}), f32[128,128]{1,0:T(8,128)}) %all-reduce.5.cloned.1.call-update) | async-done | bytes 65552 | tf_op jit(solution)/shard_map/psum | solution.py:36
  463.8 1.3 constant_dynamic-slice_fusion.1
  (3 shorter events, 0.0 us)
Async XLA Ops:
  19.2 177.2 %all-to-all-start = ((f32[1536,12,128]{2,1,0:T(8,128)}), f32[1536,12,128]{2,1,0:T(8,128)}, u32[]{:S(2)}, u32[]{:S(2)}) async-start(f32[1536,12,128]{2,1,0:T(8,128)} %copy.7), calls=%async_computation | async-start | bytes 25165824 | tf_op jit(solution)/shard_map/all_to_all | solution.py:13
  31.1 361.0 %all-reduce.3.cloned.1.call-start = ((), (), s32[]{:S(2)}) async-start(), calls=%async_computation.1 | async-start | bytes 131072 | tf_op jit(solution)/shard_map/psum | solution.py:36
  233.2 0.6 copy-start
  233.9 229.9 %all-reduce.5.cloned.1.call-start = ((), (), s32[]{:S(2)}) async-start(), calls=%async_computation.2 | async-start | bytes 131072 | tf_op jit(solution)/shard_map/psum | solution.py:36
Sparse Core Ops, SparseCore 0:
  234.0 158.0 all-reduce.2
  394.7 69.0 all-reduce.4
